TPU v7x, 32 devices: a whole 2x2x4 slice. The times are simulated.
32 devices in a mesh: groups: 2 (over y), views: 4 (over z), cols: 2 (over x), sub: 2 (over core).
Axes of the slice: x: 2, y: 2, z: 4, core: 2. Of those that a mesh axis runs over, the one named last changes fastest.
Arguments:
- images: bfloat16 [32, 8, 256], P(('groups', 'views'), None, 'cols'), parts along dimension 0, may hold values from -6 to 6
- pairs: int32 [128, 2], P('groups'), parts along dimension 0, may hold values from 0 to 15, as said below
- offsets: int32 [128], P('groups'), parts along dimension 0, may hold values from 4 to 67
Outputs:
- volume: float32 [32, 64, 8, 256], P(('groups', 'views'), 'sub', None, 'cols'), parts along dimension 0
There are 2 independent parts, one for each index of `groups`. A program takes and returns all parts, laid end to end along the dimension named above; each array names one. Nothing has to cross between parts.
Inputs may be any that keep to these rules, and one draw needn't show every extreme that they name: `pairs`: rows b * 16 to (b + 1) * 16 - 1 name as first view one of views b * 4 to (b + 1) * 4 - 1. The two views of a pair differ. Among the rows of one such block, at most 8 name second views on one index of views (second view // 4), and some block reaches 8. Over all rows, at most 32 name second views on one index of views, and some index reaches 32.
All inputs are finite; a program needn't handle non-finite values.
Results may differ from a plain program's by a relative error of at most 0.00096.
Values may be sent and summed in bfloat16 or wider, within the bound.
A program may use at most 64 MiB of HBM per device.

v0:
```python
import jax
import jax.numpy as jnp
from jax import lax
from jax.sharding import PartitionSpec as P

NDISP = 64
RAD = 4
PAIRS_DEV = 16


SMOOTH = 0.01


def from_behind(block, axis, distance):
    devices = range(lax.axis_size(axis))
    route = [(i - distance, i) for i in devices if i - distance in devices]
    return lax.ppermute(block, axis, route)


def box_sum(values, radius):
    row_count = values.shape[-2]
    columns = values.shape[-1] - 2 * radius
    widths = [(0, 0)] * (values.ndim - 2) + [(radius, radius), (0, 0)]
    padded = jnp.pad(values, widths)
    row_sums = padded[..., 0:row_count, :]
    for offset_row in range(1, 2 * radius + 1):
        row_sums = row_sums + padded[..., offset_row : offset_row + row_count, :]
    column_sums = row_sums[..., 0:columns]
    for offset_col in range(1, 2 * radius + 1):
        column_sums = column_sums + row_sums[..., offset_col : offset_col + columns]
    return column_sums


def pair_costs(window, strip_cols, disp_count, radius):
    span_cols = window.shape[-1]
    shifted = jnp.stack(
        [
            strip_cols[:, disp_count - 1 - shift_index : disp_count - 1 - shift_index + span_cols]
            for shift_index in range(disp_count)
        ]
    )
    inverse = 1.0 / float((2 * radius + 1) ** 2)
    mean_first = box_sum(window, radius) * inverse
    power_first = box_sum(window * window, radius) * inverse
    mean_second = box_sum(shifted, radius) * inverse
    power_second = box_sum(shifted * shifted, radius) * inverse
    cross_term = box_sum(window[None] * shifted, radius) * inverse
    spread_first = power_first - mean_first * mean_first + SMOOTH
    spread_second = power_second - mean_second * mean_second + SMOOTH
    cost_block = 1.0 - (cross_term - mean_first * mean_second) / jnp.sqrt(
        spread_first * spread_second
    )
    return cost_block.astype(jnp.bfloat16)


def cut_strips(source, view_ids, first_cols, strip_len):

    def one_strip(view_id, first_col):
        one_tile = lax.dynamic_index_in_dim(source, view_id, 0, keepdims=False)
        return lax.dynamic_slice_in_dim(one_tile, first_col, strip_len, 1)

    return jax.vmap(one_strip)(view_ids, first_cols)


def score_items(windows, strips, disp_count):

    def score_one(members):
        return pair_costs(
            members[0].astype(jnp.float32), members[1].astype(jnp.float32), disp_count, RAD
        )

    return lax.map(score_one, (windows, strips))


def add_costs(volume, cost_blocks, targets, live_mask):
    view_count = volume.shape[0]
    selector = ((targets[None, :] == jnp.arange(view_count)[:, None]) & live_mask[None, :]).astype(
        jnp.bfloat16
    )
    summed = jnp.dot(
        selector, cost_blocks.reshape(cost_blocks.shape[0], -1), preferred_element_type=jnp.float32
    )
    return volume + summed.reshape(volume.shape)


def per_device(images, pairs, offsets):
    view_count, row_count, columns = images.shape
    blocks = lax.axis_size("views")
    slots_per = 2 * PAIRS_DEV // blocks
    my_index = lax.axis_index("views")
    per_sub = NDISP // lax.axis_size("sub")
    sub_start = lax.axis_index("sub") * per_sub
    strip_len = columns + 2 * RAD + per_sub - 1
    right_rim = from_behind(images[:, :, :RAD], "cols", -1)
    left_tiles = []
    current = images
    for repeat in range(2):
        current = from_behind(current, "cols", 1)
        left_tiles.append(current)
    wide_tiles = jnp.concatenate([left_tiles[1], left_tiles[0], images], axis=2)
    framed = jnp.concatenate([left_tiles[0][:, :, columns - RAD :], images, right_rim], axis=2)
    pair_table = pairs.reshape(blocks, PAIRS_DEV, 2)
    shifts = offsets.reshape(blocks, PAIRS_DEV)
    first_local = pair_table[:, :, 0] % view_count
    second_owner = pair_table[:, :, 1] // view_count
    second_local = pair_table[:, :, 1] % view_count
    positions = jnp.arange(PAIRS_DEV)
    earlier = positions[None, :] < positions[:, None]
    rank_in = jnp.sum(
        ((second_owner[:, :, None] == second_owner[:, None, :]) & earlier[None]).astype(jnp.int32),
        axis=2,
    )
    slot_ids = jnp.arange(slots_per)
    block_ids = jnp.arange(blocks)
    incoming = (second_owner[:, None, :] == my_index) & (
        rank_in[:, None, :] == slot_ids[None, :, None]
    )
    in_live = jnp.any(incoming, axis=2).reshape(-1)
    in_local = jnp.sum(jnp.where(incoming, second_local[:, None, :], 0), axis=2).reshape(-1)
    my_first = first_local[my_index]
    my_owner = second_owner[my_index]
    my_rank = rank_in[my_index]
    my_shift = shifts[my_index]
    outgoing = (my_owner[None, None, :] == block_ids[:, None, None]) & (
        my_rank[None, None, :] == slot_ids[None, :, None]
    )
    out_item = jnp.sum(jnp.where(outgoing, positions[None, None, :], 0), axis=2).reshape(-1)
    windows = framed[my_first]
    gathered = lax.all_gather(wide_tiles, "views", axis=0, tiled=True)
    my_strips = cut_strips(
        gathered,
        pair_table[my_index, :, 1],
        2 * columns - RAD - my_shift - sub_start - per_sub + 1,
        strip_len,
    )
    cost_blocks = score_items(windows, my_strips, per_sub)
    volume = jnp.zeros((view_count, per_sub, row_count, columns), jnp.float32)
    volume = add_costs(volume, cost_blocks, my_first, positions >= 0)
    returned_slots = cost_blocks[out_item].reshape(blocks, slots_per, per_sub, row_count, columns)
    returned = lax.all_to_all(returned_slots, "views", split_axis=0, concat_axis=0, tiled=True)
    volume = add_costs(
        volume, returned.reshape(blocks * slots_per, per_sub, row_count, columns), in_local, in_live
    )
    return volume


def solution(mesh):
    return jax.shard_map(
        per_device,
        mesh=mesh,
        in_specs=(P(("groups", "views"), None, "cols"), P("groups", None), P("groups")),
        out_specs=P(("groups", "views"), "sub", None, "cols"),
        check_vma=False,
    )
```

profile of v0, /device:TPU:0, one launch (start us, length us, event | category | flops | bytes accessed | tf_op | source)
XLA Modules:
  0.0 157.7 jit_solution(12804099480591400244)
XLA Ops:
  0.0 4.8 %collective-permute-start = (bf16[4,8,128]{2,1,0:T(8,128)(2,1)}, bf16[4,8,128]{2,1,0:T(8,128)(2,1)S(1)}, u32[]{:S(2)}, u32[]{:S(2)}) collective-permute-start(bf16[4,8,128]{2,1,0:T(8,128)(2,1)} %param.5), channel_id=1, source_target_pairs={{0,2},{1,3},{4,6},{5,7},{8,10},{9,11},{12,14},{13,15},{16,18},{17,... | collective-permute-start | bytes 24584 | tf_op jit(solution)/shard_map/ppermute | solution.py:17
  4.8 1.3 collective-permute-start.1
  6.2 0.8 reshape.264
  7.0 0.7 reshape.265
  8.4 4.5 %collective-permute-start.2 = (bf16[4,8,128]{2,1,0:T(8,128)(2,1)S(1)}, bf16[4,8,128]{2,1,0:T(8,128)(2,1)S(1)}, u32[]{:S(2)}, u32[]{:S(2)}) collective-permute-start(bf16[4,8,128]{2,1,0:T(8,128)(2,1)S(1)} %collective-permute-done), channel_id=1, source_target_pairs={{0,2},{1,3},{4,6},{5,7},{8,10},{9,11},{12,14},{13,15},{16,18},{17,... | collective-permute-start | bytes 24584 | tf_op jit(solution)/shard_map/ppermute | solution.py:17
  12.9 0.8 pad_maximum_fusion.1
  13.7 0.6 gather_fusion
  14.3 0.7 pad_maximum_fusion
  15.0 13.6 %all_gather.3 = bf16[16,8,384]{2,1,0:T(8,128)(2,1)S(1)} all-gather(bf16[4,8,384]{2,1,0:T(8,128)(2,1)S(1)} %pad_maximum_fusion), channel_id=1, replica_groups=mesh['groups'=2,'views'=4,'cols'=2,'sub'=2] {'views'}, dimensions={0}, use_global_device_ids=true | all-gather | bytes 122880 | tf_op jit(solution)/shard_map/all_gather | solution.py:129
  28.6 0.6 gather_fusion.1
  29.2 1.2 copy.17
  30.4 2.6 %gather_fusion.3 = bf16[16,8,167]{1,0,2:T(8,128)(2,1)S(1)} fusion(bf16[16,8,384]{1,0,2:T(8,128)(2,1)S(1)} %copy.17, s32[16]{0:T(128)S(1)} %or_bitcast_fusion), kind=kCustom, calls=%fused_computation.3 | custom fusion | bytes 85696 | tf_op jit(solution)/shard_map/vmap()/gather | solution.py:60
  33.0 0.6 copy.18
  33.5 66.2 %while.12 = (s32[]{:T(128)}, bf16[16,32,8,128]{3,2,1,0:T(8,128)(2,1)S(1)}, bf16[16,8,136]{2,1,0:T(8,128)(2,1)S(1)}, bf16[16,8,167]{2,1,0:T(8,128)(2,1)S(1)}, s32[]{:T(128)}) while((s32[]{:T(128)}, bf16[16,32,8,128]{3,2,1,0:T(8,128)(2,1)S(1)}, bf16[16,8,136]{2,1,0:T(8,128)(2,1)S(1)}, bf16[16,8,167]{2,1,0:T(8,128)(2,1)S(1)}, s32[]{:T(128)}) %tuple.44), condition=%wide.region_1.2_spmd, body=%wide.region_0.1_spmd.sunk | while | flops 2129402 | bytes 5380261 | solution.py:72
  36.3 0.4 fusion.91
  36.7 0.9 bitcast_dynamic-update-slice_fusion.2
  40.5 0.4 fusion.91
  40.9 0.9 bitcast_dynamic-update-slice_fusion.2
  44.6 0.4 fusion.91
  45.0 0.9 bitcast_dynamic-update-slice_fusion.2
  48.7 0.4 fusion.91
  49.2 0.9 bitcast_dynamic-update-slice_fusion.2
  52.9 0.4 fusion.91
  53.3 0.9 bitcast_dynamic-update-slice_fusion.2
  57.0 0.4 fusion.91
  57.5 0.9 bitcast_dynamic-update-slice_fusion.2
  61.2 0.4 fusion.91
  61.6 0.9 bitcast_dynamic-update-slice_fusion.2
  65.3 0.4 fusion.91
  65.7 0.9 bitcast_dynamic-update-slice_fusion.2
  69.4 0.4 fusion.91
  69.9 0.9 bitcast_dynamic-update-slice_fusion.2
  74.0 0.9 bitcast_dynamic-update-slice_fusion.2
  78.2 0.9 bitcast_dynamic-update-slice_fusion.2
  82.3 0.9 bitcast_dynamic-update-slice_fusion.2
  86.4 0.9 bitcast_dynamic-update-slice_fusion.2
  90.6 0.9 bitcast_dynamic-update-slice_fusion.2
  94.7 0.9 bitcast_dynamic-update-slice_fusion.2
  98.9 0.9 bitcast_dynamic-update-slice_fusion.2
  99.8 2.2 %gather_fusion.2 = bf16[32,32,8,128]{3,2,1,0:T(8,128)(2,1)} fusion(bf16[16,32,8,128]{3,2,1,0:T(8,128)(2,1)S(1)} %get-tuple-element.59, s32[1024]{0:T(1024)S(1)} %pad_clamp_fusion), kind=kCustom, calls=%fused_computation.2 | custom fusion | bytes 4194432 | tf_op jit(solution)/shard_map/gather | solution.py:139
  101.9 4.6 %all-to-all-start = ((bf16[4,8,32,8,128]{4,3,2,1,0:T(8,128)(2,1)}), bf16[4,8,32,8,128]{4,3,2,1,0:T(8,128)(2,1)S(1)}, u32[]{:S(2)}, u32[]{:S(2)}) async-start(bf16[4,8,32,8,128]{4,3,2,1,0:T(8,128)(2,1)} %bitcast.304), calls=%async_computation | async-start | bytes 4194304 | tf_op jit(solution)/shard_map/all_to_all | solution.py:140
  107.0 0.7 copy.34
  107.9 1.5 fusion.59
  109.4 41.8 %all-to-all-done = bf16[4,8,32,8,128]{4,3,2,1,0:T(8,128)(2,1)S(1)} async-done(((bf16[4,8,32,8,128]{4,3,2,1,0:T(8,128)(2,1)}), bf16[4,8,32,8,128]{4,3,2,1,0:T(8,128)(2,1)S(1)}, u32[]{:S(2)}, u32[]{:S(2)}) %all-to-all-start) | async-done | bytes 2097184 | tf_op jit(solution)/shard_map/all_to_all | solution.py:140
  151.2 2.3 %reshape_reshape.3 = bf16[32,32768]{1,0:T(8,128)(2,1)} reshape(bf16[4,8,32,8,128]{4,3,2,1,0:T(8,128)(2,1)S(1)} %all-to-all-done) | data formatting | bytes 4194304 | tf_op jit(solution)/shard_map/reshape;reshape | solution.py:81
  153.5 2.1 %copy.26 = bf16[4,8,256,128]{3,2,1,0:T(8,128)(2,1)S(1)} copy(bf16[4,8,256,128]{3,1,2,0:T(8,128)(2,1)} %bitcast.306) | data formatting | bytes 4194304
  155.6 1.3 fusion.56
  156.9 0.8 copy.21
  (676 shorter events, 48.0 us)
Async XLA Ops:
  0.0 8.3 %collective-permute-start = (bf16[4,8,128]{2,1,0:T(8,128)(2,1)}, bf16[4,8,128]{2,1,0:T(8,128)(2,1)S(1)}, u32[]{:S(2)}, u32[]{:S(2)}) collective-permute-start(bf16[4,8,128]{2,1,0:T(8,128)(2,1)} %param.5), channel_id=1, source_target_pairs={{0,2},{1,3},{4,6},{5,7},{8,10},{9,11},{12,14},{13,15},{16,18},{17,... | collective-permute-start | bytes 24584 | tf_op jit(solution)/shard_map/ppermute | solution.py:17
  4.8 8.1 %collective-permute-start.1 = (bf16[4,8,4]{2,1,0:T(8,128)(2,1)}, bf16[4,8,4]{2,1,0:T(8,128)(2,1)S(1)}, u32[]{:S(2)}, u32[]{:S(2)}) collective-permute-start(bf16[4,8,4]{2,1,0:T(8,128)(2,1)} %bitcast.308), channel_id=1, source_target_pairs={{2,0},{3,1},{6,4},{7,5},{10,8},{11,9},{14,12},{15,13},{18,16},{19,... | collective-permute-start | bytes 776 | tf_op jit(solution)/shard_map/ppermute | solution.py:17
  8.4 5.9 %collective-permute-start.2 = (bf16[4,8,128]{2,1,0:T(8,128)(2,1)S(1)}, bf16[4,8,128]{2,1,0:T(8,128)(2,1)S(1)}, u32[]{:S(2)}, u32[]{:S(2)}) collective-permute-start(bf16[4,8,128]{2,1,0:T(8,128)(2,1)S(1)} %collective-permute-done), channel_id=1, source_target_pairs={{0,2},{1,3},{4,6},{5,7},{8,10},{9,11},{12,14},{13,15},{16,18},{17,... | collective-permute-start | bytes 24584 | tf_op jit(solution)/shard_map/ppermute | solution.py:17
  101.9 49.2 %all-to-all-start = ((bf16[4,8,32,8,128]{4,3,2,1,0:T(8,128)(2,1)}), bf16[4,8,32,8,128]{4,3,2,1,0:T(8,128)(2,1)S(1)}, u32[]{:S(2)}, u32[]{:S(2)}) async-start(bf16[4,8,32,8,128]{4,3,2,1,0:T(8,128)(2,1)} %bitcast.304), calls=%async_computation | async-start | bytes 4194304 | tf_op jit(solution)/shard_map/all_to_all | solution.py:140
  153.5 2.1 %copy-start = (f32[4,32,8,128]{3,0,2,1:T(4,128)S(1)}, f32[4,32,8,128]{3,0,2,1:T(4,128)}, u32[]{:S(2)}) copy-start(f32[4,32,8,128]{3,0,2,1:T(4,128)} %fusion.59) | copy-start | bytes 1572868
where the time goes:
time: 158 us
  local copies, waits for them, and re-layouts  51.4 us (33%)
  waiting for transfers between devices  41.8 us (26%)
  other arithmetic  31.6 us (20%)
  starting transfers between devices  15.3 us (10%)
  blocking collectives  13.6 us (9%)
  matrix products  2.76 us (2%)
    all_to_all x1, waiting for transfers between devices, per_device(): lax.all_to_all(returned_slots, 'views', split_axis=0, concat_axis=0, tile...  41.8 us
    while x496, local copies, waits for them, and re-layouts  35.8 us
    dynamic_update_slice x16, other arithmetic, score_items(): return lax.map(score_one, (windows, strips))  14.7 us
    all_gather x1, blocking collectives, per_device(): gathered = lax.all_gather(wide_tiles, 'views', axis=0, tiled=True)  13.6 us
    ppermute x3, starting transfers between devices, from_behind(): return lax.ppermute(block, axis, route)  10.7 us
    add x48, other arithmetic, box_sum(): row_sums = row_sums + padded[..., offset_row:offset_row + row_count, :]  7.27 us
    mul x32, other arithmetic, pair_costs(): cross_term = box_sum(window[None] * shifted, radius) * inverse  4.68 us
    all_to_all x1, starting transfers between devices, per_device(): lax.all_to_all(returned_slots, 'views', split_axis=0, concat_axis=0, tile...  4.6 us
  transfers between devices with their start and end apart: 4, of which 1 were waited for; matrix products, arithmetic and copies ran while one was open for 4% of the time, Pallas kernels for 0%

commit v1 on v0

v1 whole, which is shorter than its diff:
```python
import functools

import jax
import jax.numpy as jnp
from jax import lax
from jax.experimental import pallas as pl
from jax.experimental.pallas import tpu as pltpu
from jax.sharding import PartitionSpec as P

NDISP = 64
RAD = 4
SMOOTH = 0.01
LANES = 128
WIN = 2 * RAD + 1
MESH = pl.DeviceIdType.MESH


def gather_kernel(blocks, cols, x_ref, out_ref, send_sem, recv_sem, own_sem):
    my_view = lax.axis_index("views")
    my_col = lax.axis_index("cols")
    me = my_view * cols + my_col
    total = blocks * cols

    def peer(step):
        other = lax.rem(me + step, total)
        return {"views": other // cols, "cols": lax.rem(other, cols)}

    own = pltpu.make_async_copy(x_ref, out_ref.at[my_col, my_view], own_sem)
    own.start()
    barrier = pltpu.get_barrier_semaphore()
    for step in range(1, total):
        pl.semaphore_signal(barrier, inc=1, device_id=peer(step), device_id_type=MESH)
    pl.semaphore_wait(barrier, total - 1)
    copies = []
    for step in range(1, total):
        copy = pltpu.make_async_remote_copy(
            src_ref=x_ref,
            dst_ref=out_ref.at[my_col, my_view],
            send_sem=send_sem.at[step],
            recv_sem=recv_sem.at[step],
            device_id=peer(step),
            device_id_type=MESH,
        )
        copy.start()
        copies.append(copy)
    own.wait()
    for copy in copies:
        copy.wait()


def gather_images(images, blocks, cols):
    rows, columns = images.shape
    total = blocks * cols
    return pl.pallas_call(
        functools.partial(gather_kernel, blocks, cols),
        out_shape=jax.ShapeDtypeStruct((cols, blocks, rows, columns), images.dtype),
        in_specs=[pl.BlockSpec(memory_space=pltpu.VMEM)],
        out_specs=pl.BlockSpec(memory_space=pltpu.VMEM),
        scratch_shapes=[
            pltpu.SemaphoreType.DMA((total,)),
            pltpu.SemaphoreType.DMA((total,)),
            pltpu.SemaphoreType.DMA,
        ],
        compiler_params=pltpu.CompilerParams(collective_id=0, has_side_effects=True),
    )(images)


def split_exact(values):
    high = values.astype(jnp.bfloat16)
    low = (values - high.astype(jnp.float32)).astype(jnp.bfloat16)
    return high, low


def cost_kernel(
    dims, gath_ref, pairs_ref, offs_ref, out_ref,
    nat, nat_f, nat_m, nat_r, st_g, st_m, st_r, st_f, st_a, st_b,
    gt, m2t, r2t, ft, m1t, r1t, sel, box, two, four, task_ref,
):
    blocks, cols, views, rows, columns, pair_count, per_sub, batches = dims
    per_batch = LANES // rows
    per_block = pair_count // blocks
    all_rows = blocks * views * rows
    wide = 4 * columns
    my_view = lax.axis_index("views")
    my_col = lax.axis_index("cols")
    sub_start = lax.axis_index("sub") * per_sub
    scale = 1.0 / float(WIN * WIN)

    def clear(slot, carry):
        task_ref[slot] = -1
        return carry

    lax.fori_loop(per_block, batches * per_batch, clear, 0)
    for slot in range(per_block):
        task_ref[slot] = my_view * per_block + slot

    def list_pair(pair, count):
        first = pairs_ref[2 * pair] // views
        second = pairs_ref[2 * pair + 1] // views
        take = (second == my_view) & (first != my_view)

        @pl.when(take)
        def _():
            task_ref[count] = pair

        return count + take.astype(jnp.int32)

    lax.fori_loop(0, pair_count, list_pair, jnp.int32(per_block))

    for place in range(4):
        index = my_col + (place - 2)
        ok = (index >= 0) & (index < cols)
        block = gath_ref[jnp.clip(index, 0, cols - 1)]
        block = block.reshape(all_rows, columns).astype(jnp.float32)
        nat[:, place * columns : (place + 1) * columns] = jnp.where(ok, block, 0.0)

    row_of = lax.broadcasted_iota(jnp.int32, (LANES, LANES), 0)
    lane_of = lax.broadcasted_iota(jnp.int32, (LANES, LANES), 1)
    band = (
        ((row_of // rows) == (lane_of // rows)) & (jnp.abs(row_of - lane_of) <= RAD)
    ).astype(jnp.bfloat16)
    band_wide = jnp.concatenate([band, band], axis=1)
    band_tall = jnp.concatenate([band, band], axis=0)

    def across(sums):
        pair_sum = sums + pltpu.roll(sums, 1, 1)
        quad = pair_sum + pltpu.roll(pair_sum, 2, 1)
        octo = quad + pltpu.roll(quad, 4, 1)
        return pltpu.roll(octo + pltpu.roll(sums, 8, 1), wide - RAD, 1)

    for chunk in range(all_rows // LANES):
        span = slice(chunk * LANES, (chunk + 1) * LANES)
        tile = nat[span, :]
        nat_f[span, :] = pltpu.roll(tile, 2 * columns + RAD, 1)[:, : 2 * columns]
        mean = across(
            jnp.dot(band, tile.astype(jnp.bfloat16), preferred_element_type=jnp.float32)
        ) * scale
        high, low = split_exact(tile * tile)
        power = across(
            jnp.dot(
                band_wide, jnp.concatenate([high, low], axis=0), preferred_element_type=jnp.float32
            )
        ) * scale
        nat_m[span, :] = mean
        nat_r[span, :] = lax.rsqrt(power - mean * mean + SMOOTH)

    slot_lane = lax.broadcasted_iota(jnp.int32, (views * rows, LANES), 1)
    view_row = lax.broadcasted_iota(jnp.int32, (views * rows, LANES), 0)

    def prepare(batch, carry):
        first_of = jnp.full((views * rows, LANES), -1, jnp.int32)
        second_of = first_of
        for slot in range(per_batch):
            pair = task_ref[batch * per_batch + slot]
            live = pair >= 0
            pair = jnp.maximum(pair, 0)
            first = pairs_ref[2 * pair]
            second = pairs_ref[2 * pair + 1]
            shift = offs_ref[pair]
            first_at = pl.ds(pl.multiple_of(first * rows, rows), rows)
            second_at = pl.ds(pl.multiple_of(second * rows, rows), rows)
            here = slice(slot * rows, (slot + 1) * rows)
            start = 2 * columns - per_sub - RAD - shift - sub_start
            turn = wide - start
            st_g[here, :] = pltpu.roll(nat[second_at, :], turn, 1)[:, : 2 * columns]
            st_m[here, :] = pltpu.roll(nat_m[second_at, :], turn, 1)[:, : 2 * columns]
            st_r[here, :] = pltpu.roll(nat_r[second_at, :], turn, 1)[:, : 2 * columns]
            st_f[here, :] = nat_f[first_at, :]
            st_a[here, :] = nat_m[first_at, 2 * columns : 3 * columns]
            st_b[here, :] = nat_r[first_at, 2 * columns : 3 * columns]
            mine = (slot_lane // rows) == slot
            base = my_view * views
            first_of = jnp.where(mine, jnp.where(live, first - base, -1), first_of)
            second_of = jnp.where(mine, jnp.where(live, second - base, -1), second_of)
        target = view_row // rows
        same_row = lax.rem(slot_lane, rows) == lax.rem(view_row, rows)
        hit = ((first_of == target) | (second_of == target)) & same_row
        sel[batch] = hit.astype(jnp.bfloat16)
        gt[batch] = st_g[...].T
        m2t[batch] = st_m[...].T
        r2t[batch] = st_r[...].T
        ft[batch] = st_f[...].T
        m1t[batch] = st_a[...].T * float(WIN * WIN)
        r1t[batch] = st_b[...].T * scale
        return carry

    lax.fori_loop(0, batches, prepare, 0)

    span = columns + 2 * RAD

    def score(disp, carry):
        summed = jnp.zeros((views * rows, columns), jnp.float32)
        for batch in range(batches):
            product = ft[batch, 0:span, :] * gt[batch, pl.ds(per_sub - disp, span), :]
            high, low = split_exact(product)
            sums = jnp.dot(
                jnp.concatenate([high, low], axis=1), band_tall, preferred_element_type=jnp.float32
            )
            box[batch, 0:span, :] = sums
            two[batch, 0:span, :] = sums + box[batch, 1 : span + 1, :]
            four[batch, 0:span, :] = two[batch, 0:span, :] + two[batch, 2 : span + 2, :]
            cross = (
                four[batch, 0:columns, :] + four[batch, 4 : columns + 4, :]
                + box[batch, 8 : columns + 8, :]
            )
            at = pl.ds(per_sub + RAD - disp, columns)
            gain = r1t[batch] * r2t[batch, at, :]
            cost = 1.0 - (cross - m1t[batch] * m2t[batch, at, :]) * gain
            summed = summed + lax.dot_general(
                sel[batch], cost.astype(jnp.bfloat16), (((1,), (1,)), ((), ())),
                preferred_element_type=jnp.float32,
            )
        out_ref[:, disp] = summed.reshape(views, rows, columns)
        return carry

    lax.fori_loop(0, per_sub, score, 0)


def per_device(images, pairs, offsets):
    views, rows, columns = images.shape
    blocks = lax.axis_size("views")
    cols = lax.axis_size("cols")
    per_sub = NDISP // lax.axis_size("sub")
    pair_count = pairs.shape[0]
    per_block = pair_count // blocks
    arriving = (2 * per_block // blocks) * (blocks - 1)
    per_batch = LANES // rows
    batches = -(-(per_block + arriving) // per_batch)
    gathered = gather_images(images.reshape(views * rows, columns), blocks, cols)
    dims = (blocks, cols, views, rows, columns, pair_count, per_sub, batches)
    all_rows = blocks * views * rows
    span = columns + 2 * RAD
    f32 = jnp.float32
    stage = pltpu.VMEM((LANES, 2 * columns), f32)
    narrow = pltpu.VMEM((LANES, columns), f32)
    turned = pltpu.VMEM((batches, 2 * columns, LANES), f32)
    turned_narrow = pltpu.VMEM((batches, columns, LANES), f32)
    work = pltpu.VMEM((batches, span + 8, LANES), f32)
    whole = pltpu.VMEM((all_rows, 4 * columns), f32)
    smem = pl.BlockSpec(memory_space=pltpu.SMEM)
    vmem = pl.BlockSpec(memory_space=pltpu.VMEM)
    return pl.pallas_call(
        functools.partial(cost_kernel, dims),
        out_shape=jax.ShapeDtypeStruct((views, per_sub, rows, columns), f32),
        in_specs=[vmem, smem, smem],
        out_specs=vmem,
        scratch_shapes=[
            whole, pltpu.VMEM((all_rows, 2 * columns), f32), whole, whole,
            stage, stage, stage, stage, narrow, narrow,
            turned, turned, turned, turned, turned_narrow, turned_narrow,
            pltpu.VMEM((batches, views * rows, LANES), jnp.bfloat16),
            work, work, work,
            pltpu.SMEM((batches * per_batch,), jnp.int32),
        ],
        compiler_params=pltpu.CompilerParams(vmem_limit_bytes=40 * 2**20),
    )(gathered, pairs.reshape(-1), offsets)


def solution(mesh):
    return jax.shard_map(
        per_device,
        mesh=mesh,
        in_specs=(P(("groups", "views"), None, "cols"), P("groups", None), P("groups")),
        out_specs=P(("groups", "views"), "sub", None, "cols"),
        check_vma=False,
    )
```

time: 158 us -> 30.8 us (0.19)
  local copies, waits for them, and re-layouts: 51.4 us -> 1.75 us
  waiting for transfers between devices: 41.8 us -> 0 us
  other arithmetic: 31.6 us -> 0 us
  Pallas kernels: 0 us -> 28.8 us
  starting transfers between devices: 15.3 us -> 0 us
  blocking collectives: 13.6 us -> 0 us
  matrix products: 2.76 us -> 0 us
    all_to_all x1 -> x0, waiting for transfers between devices: 41.8 us -> none  [per_device(): lax.all_to_all(returned_slots, 'views', split_axis=0, concat_axis=0, tile...]
    while x497 -> x0, local copies, waits for them, and re-layouts: 36.4 us -> none
    pallas_call x0 -> x2, Pallas kernels: none -> 28.8 us  [the longest x1 18.8 us: per_device(): pl.pallas_call(functools.partial(cost_kernel, dims), out_shape=jax.ShapeD...]
    dynamic_update_slice x16 -> x0, other arithmetic: 14.7 us -> none  [score_items(): return lax.map(score_one, (windows, strips))]
    all_gather x1 -> x0, blocking collectives: 13.6 us -> none  [per_device(): gathered = lax.all_gather(wide_tiles, 'views', axis=0, tiled=True)]
    ppermute x3 -> x0, starting transfers between devices: 10.7 us -> none  [from_behind(): return lax.ppermute(block, axis, route)]
    add x64 -> x0, other arithmetic: 8.57 us -> none  [the longest x48 7.27 us: box_sum(): row_sums = row_sums + padded[..., offset_row:offset_row + row_count, :]]
    gather x5 -> x0, local copies, waits for them, and re-layouts: 7.1 us -> none  [the longest x1 2.59 us: one_strip(): return lax.dynamic_slice_in_dim(one_tile, first_col, strip_len, 1)]
  transfers between devices with their start and end apart: 4 -> 0, of which waited for: 1 -> 0; matrix products, arithmetic and copies ran while one was open for 4% -> 0% of each run, Pallas kernels for 0% -> 0%
where the time goes in v1:
time: 30.8 us; the launch traced here: 30.6 us
  Pallas kernels  28.8 us (94%)
  local copies, waits for them, and re-layouts  1.75 us (6%)
    pallas_call x1, Pallas kernels, per_device(): pl.pallas_call(functools.partial(cost_kernel, dims), out_shape=jax.ShapeD...  18.8 us
    pallas_call x1, Pallas kernels, gather_images(): pl.pallas_call(functools.partial(gather_kernel, blocks, cols), out_shape=...  10 us
    unnamed x7, local copies, waits for them, and re-layouts  1.61 us

profile of v1, /device:TPU:0, one launch (start us, length us, event | category | flops | bytes accessed | tf_op | source)
XLA Modules:
  0.0 30.6 jit_solution(7014471368347909257)
XLA Ops:
  0.0 0.0 copy-start.2
  0.0 0.7 %copy-done.2 = s32[64,2]{0,1:T(2,128)S(1)} copy-done((s32[64,2]{0,1:T(2,128)S(1)}, s32[64,2]{0,1:T(2,128)}, u32[]{:S(2)}) %copy-start.2) | copy-done | bytes 536
  0.7 0.1 copy.5
  0.8 0.1 reshape.7.pairs_ref
  0.9 0.0 copy-start.1
  0.9 10.0 %shard_map.37.gath_ref = bf16[2,4,32,128]{3,2,1,0:T(8,128)(2,1)} custom-call(bf16[32,128]{1,0:T(8,128)(2,1)} %bitcast.1), custom_call_target="tpu_custom_call" | custom-call | tf_op jit(solution)/shard_map/pallas_call | solution.py:54
  10.9 0.0 copy-done.1
  11.0 0.0 copy-start
  11.0 0.8 %copy-done = bf16[2,4,32,128]{3,2,1,0:T(8,128)(2,1)S(1)} copy-done((bf16[2,4,32,128]{3,2,1,0:T(8,128)(2,1)S(1)}, bf16[2,4,32,128]{3,2,1,0:T(8,128)(2,1)}, u32[]{:S(2)}) %copy-start) | copy-done | bytes 65560
  11.8 18.8 %shard_map.38 = f32[4,32,8,128]{3,2,1,0:T(8,128)} custom-call(bf16[2,4,32,128]{3,2,1,0:T(8,128)(2,1)S(1)} %copy-done, s32[128]{0:T(128)S(1)} %reshape.7.pairs_ref, s32[64]{0:T(128)S(1)} %copy-done.1), custom_call_target="tpu_custom_call" | custom-call | tf_op jit(solution)/shard_map/pallas_call | solution.py:242
Async XLA Ops:
  0.0 0.7 %copy-start.2 = (s32[64,2]{0,1:T(2,128)S(1)}, s32[64,2]{0,1:T(2,128)}, u32[]{:S(2)}) copy-start(s32[64,2]{0,1:T(2,128)} %param.4) | copy-start | bytes 1540
  0.9 10.0 %copy-start.1 = (s32[64]{0:T(128)S(1)}, s32[64]{0:T(128)}, u32[]{:S(2)}) copy-start(s32[64]{0:T(128)} %offs_ref.1) | copy-start | bytes 772
  11.0 0.8 %copy-start = (bf16[2,4,32,128]{3,2,1,0:T(8,128)(2,1)S(1)}, bf16[2,4,32,128]{3,2,1,0:T(8,128)(2,1)}, u32[]{:S(2)}) copy-start(bf16[2,4,32,128]{3,2,1,0:T(8,128)(2,1)} %shard_map.37.gath_ref) | copy-start | bytes 196612

commit v2 on v1

--- a/solution.py
+++ b/solution.py
@@ -11,6 +11,7 @@
 RAD = 4
 SMOOTH = 0.01
 LANES = 128
+FOLD = 2
 WIN = 2 * RAD + 1
 MESH = pl.DeviceIdType.MESH
 
@@ -76,9 +77,10 @@
     nat, nat_f, nat_m, nat_r, st_g, st_m, st_r, st_f, st_a, st_b,
     gt, m2t, r2t, ft, m1t, r1t, sel, box, two, four, task_ref,
 ):
-    blocks, cols, views, rows, columns, pair_count, per_sub, batches = dims
+    blocks, cols, views, rows, columns, pair_count, per_sub, batches, folded = dims
     per_batch = LANES // rows
     per_block = pair_count // blocks
+    slots = batches * per_batch
     all_rows = blocks * views * rows
     wide = 4 * columns
     my_view = lax.axis_index("views")
@@ -86,26 +88,25 @@
     sub_start = lax.axis_index("sub") * per_sub
     scale = 1.0 / float(WIN * WIN)
 
+    base = my_view * views
+    for slot in range(per_block):
+        task_ref[slot] = my_view * per_block + slot
+
+    def is_mine(view):
+        return (view >= base) & (view < base + views)
+
+    def list_pair(pair, count):
+        take = is_mine(pairs_ref[1, pair]) & jnp.logical_not(is_mine(pairs_ref[0, pair]))
+        task_ref[count] = pair
+        return count + take.astype(jnp.int32)
+
+    listed = lax.fori_loop(0, pair_count, list_pair, jnp.int32(per_block), unroll=8)
+
     def clear(slot, carry):
         task_ref[slot] = -1
         return carry
 
-    lax.fori_loop(per_block, batches * per_batch, clear, 0)
-    for slot in range(per_block):
-        task_ref[slot] = my_view * per_block + slot
-
-    def list_pair(pair, count):
-        first = pairs_ref[2 * pair] // views
-        second = pairs_ref[2 * pair + 1] // views
-        take = (second == my_view) & (first != my_view)
-
-        @pl.when(take)
-        def _():
-            task_ref[count] = pair
-
-        return count + take.astype(jnp.int32)
-
-    lax.fori_loop(0, pair_count, list_pair, jnp.int32(per_block))
+    lax.fori_loop(listed, slots + 1, clear, 0)
 
     for place in range(4):
         index = my_col + (place - 2)
@@ -147,73 +148,102 @@
     slot_lane = lax.broadcasted_iota(jnp.int32, (views * rows, LANES), 1)
     view_row = lax.broadcasted_iota(jnp.int32, (views * rows, LANES), 0)
 
-    def prepare(batch, carry):
+    half = per_sub // 2
+    three = 3 * columns
+    target = view_row // rows
+    same_row = lax.rem(slot_lane, rows) == lax.rem(view_row, rows)
+
+    def prepare(batch, fold):
         first_of = jnp.full((views * rows, LANES), -1, jnp.int32)
         second_of = first_of
         for slot in range(per_batch):
-            pair = task_ref[batch * per_batch + slot]
+            late = fold and 2 * slot >= per_batch
+            pair = task_ref[batch * per_batch + (slot - per_batch // 2 if late else slot)]
             live = pair >= 0
             pair = jnp.maximum(pair, 0)
-            first = pairs_ref[2 * pair]
-            second = pairs_ref[2 * pair + 1]
-            shift = offs_ref[pair]
+            first = pairs_ref[0, pair]
+            second = pairs_ref[1, pair]
             first_at = pl.ds(pl.multiple_of(first * rows, rows), rows)
             second_at = pl.ds(pl.multiple_of(second * rows, rows), rows)
             here = slice(slot * rows, (slot + 1) * rows)
-            start = 2 * columns - per_sub - RAD - shift - sub_start
-            turn = wide - start
-            st_g[here, :] = pltpu.roll(nat[second_at, :], turn, 1)[:, : 2 * columns]
-            st_m[here, :] = pltpu.roll(nat_m[second_at, :], turn, 1)[:, : 2 * columns]
-            st_r[here, :] = pltpu.roll(nat_r[second_at, :], turn, 1)[:, : 2 * columns]
+            start = 2 * columns - per_sub - RAD - offs_ref[pair] - sub_start
+            if late:
+                start = start - half
+            turn = three - start
+            st_g[here, :] = pltpu.roll(nat[second_at, :three], turn, 1)[:, : 2 * columns]
+            st_m[here, :] = pltpu.roll(nat_m[second_at, :three], turn, 1)[:, : 2 * columns]
+            st_r[here, :] = pltpu.roll(nat_r[second_at, :three], turn, 1)[:, : 2 * columns]
             st_f[here, :] = nat_f[first_at, :]
-            st_a[here, :] = nat_m[first_at, 2 * columns : 3 * columns]
-            st_b[here, :] = nat_r[first_at, 2 * columns : 3 * columns]
+            st_a[here, :] = nat_m[first_at, 2 * columns : three]
+            st_b[here, :] = nat_r[first_at, 2 * columns : three]
             mine = (slot_lane // rows) == slot
-            base = my_view * views
             first_of = jnp.where(mine, jnp.where(live, first - base, -1), first_of)
             second_of = jnp.where(mine, jnp.where(live, second - base, -1), second_of)
-        target = view_row // rows
-        same_row = lax.rem(slot_lane, rows) == lax.rem(view_row, rows)
         hit = ((first_of == target) | (second_of == target)) & same_row
-        sel[batch] = hit.astype(jnp.bfloat16)
+        early = slot_lane < LANES // 2
+        for part in range(2):
+            chosen = hit & (early if part == 0 else jnp.logical_not(early)) if fold else hit
+            sel[part, batch] = chosen.astype(jnp.float32).astype(jnp.bfloat16)
         gt[batch] = st_g[...].T
         m2t[batch] = st_m[...].T
         r2t[batch] = st_r[...].T
         ft[batch] = st_f[...].T
         m1t[batch] = st_a[...].T * float(WIN * WIN)
         r1t[batch] = st_b[...].T * scale
+
+    def prepare_full(batch, carry):
+        prepare(batch, False)
         return carry
 
-    lax.fori_loop(0, batches, prepare, 0)
+    lax.fori_loop(0, batches - int(folded), prepare_full, 0)
+    if folded:
+        prepare(batches - 1, True)
 
     span = columns + 2 * RAD
-
-    def score(disp, carry):
-        summed = jnp.zeros((views * rows, columns), jnp.float32)
-        for batch in range(batches):
-            product = ft[batch, 0:span, :] * gt[batch, pl.ds(per_sub - disp, span), :]
-            high, low = split_exact(product)
-            sums = jnp.dot(
-                jnp.concatenate([high, low], axis=1), band_tall, preferred_element_type=jnp.float32
-            )
-            box[batch, 0:span, :] = sums
-            two[batch, 0:span, :] = sums + box[batch, 1 : span + 1, :]
-            four[batch, 0:span, :] = two[batch, 0:span, :] + two[batch, 2 : span + 2, :]
-            cross = (
-                four[batch, 0:columns, :] + four[batch, 4 : columns + 4, :]
-                + box[batch, 8 : columns + 8, :]
-            )
+    work = [(batch, part) for part in range(2) for batch in range(batches)]
+    if folded:
+        work.remove((batches - 1, 1))
+
+    def score(step, buffer):
+        parts = []
+        for batch, part in work:
+            disp = step + part * half
+            parts.append(
+                split_exact(ft[batch, 0:span, :] * gt[batch, pl.ds(per_sub - disp, span), :])
+            )
+        stacked = jnp.concatenate([jnp.concatenate(pair, axis=1) for pair in parts], axis=0)
+        sums = jnp.dot(stacked, band_tall, preferred_element_type=jnp.float32)
+        costs = {}
+        for unit, (batch, part) in enumerate(work):
+            disp = step + part * half
+            box_at, two_at, four_at = box.at[buffer, unit], two.at[buffer, unit], four.at[buffer, unit]
+            one = sums[unit * span : (unit + 1) * span]
+            box_at[0:span, :] = one
+            pair_sum = one + box_at[1 : span + 1, :]
+            two_at[0:span, :] = pair_sum
+            quad = pair_sum + two_at[2 : span + 2, :]
+            four_at[0:span, :] = quad
+            cross = quad[0:columns] + four_at[4 : columns + 4, :] + one[2 * RAD :]
             at = pl.ds(per_sub + RAD - disp, columns)
             gain = r1t[batch] * r2t[batch, at, :]
             cost = 1.0 - (cross - m1t[batch] * m2t[batch, at, :]) * gain
-            summed = summed + lax.dot_general(
-                sel[batch], cost.astype(jnp.bfloat16), (((1,), (1,)), ((), ())),
-                preferred_element_type=jnp.float32,
-            )
-        out_ref[:, disp] = summed.reshape(views, rows, columns)
+            costs[batch, part] = cost.astype(jnp.bfloat16)
+        for part in range(2):
+            chosen = jnp.concatenate([sel[part, batch] for batch in range(batches)], axis=1)
+            whole = jnp.concatenate(
+                [costs.get((batch, part), costs[batch, 0]) for batch in range(batches)], axis=1
+            )
+            summed = lax.dot_general(
+                chosen, whole, (((1,), (1,)), ((), ())), preferred_element_type=jnp.float32
+            )
+            out_ref[:, step + part * half] = summed.reshape(views, rows, columns)
+
+    def score_steps(index, carry):
+        for buffer in range(FOLD):
+            score(index * FOLD + buffer, buffer)
         return carry
 
-    lax.fori_loop(0, per_sub, score, 0)
+    lax.fori_loop(0, half // FOLD, score_steps, 0)
 
 
 def per_device(images, pairs, offsets):
@@ -226,8 +256,10 @@
     arriving = (2 * per_block // blocks) * (blocks - 1)
     per_batch = LANES // rows
     batches = -(-(per_block + arriving) // per_batch)
+    folded = 2 * (batches * per_batch - per_block - arriving) >= per_batch
+    units = 2 * batches - int(folded)
     gathered = gather_images(images.reshape(views * rows, columns), blocks, cols)
-    dims = (blocks, cols, views, rows, columns, pair_count, per_sub, batches)
+    dims = (blocks, cols, views, rows, columns, pair_count, per_sub, batches, folded)
     all_rows = blocks * views * rows
     span = columns + 2 * RAD
     f32 = jnp.float32
@@ -235,7 +267,7 @@
     narrow = pltpu.VMEM((LANES, columns), f32)
     turned = pltpu.VMEM((batches, 2 * columns, LANES), f32)
     turned_narrow = pltpu.VMEM((batches, columns, LANES), f32)
-    work = pltpu.VMEM((batches, span + 8, LANES), f32)
+    work = pltpu.VMEM((FOLD, units, span + 8, LANES), f32)
     whole = pltpu.VMEM((all_rows, 4 * columns), f32)
     smem = pl.BlockSpec(memory_space=pltpu.SMEM)
     vmem = pl.BlockSpec(memory_space=pltpu.VMEM)
@@ -248,12 +280,12 @@
             whole, pltpu.VMEM((all_rows, 2 * columns), f32), whole, whole,
             stage, stage, stage, stage, narrow, narrow,
             turned, turned, turned, turned, turned_narrow, turned_narrow,
-            pltpu.VMEM((batches, views * rows, LANES), jnp.bfloat16),
+            pltpu.VMEM((2, batches, views * rows, LANES), jnp.bfloat16),
             work, work, work,
-            pltpu.SMEM((batches * per_batch,), jnp.int32),
+            pltpu.SMEM((batches * per_batch + 1,), jnp.int32),
         ],
         compiler_params=pltpu.CompilerParams(vmem_limit_bytes=40 * 2**20),
-    )(gathered, pairs.reshape(-1), offsets)
+    )(gathered, pairs.T, offsets)
 
 
 def solution(mesh):

time: 30.8 us -> 24.1 us (0.78)
  Pallas kernels: 28.8 us -> 23 us
  local copies, waits for them, and re-layouts: 1.75 us -> 0.84 us
    pallas_call x1, Pallas kernels: 18.8 us -> 13 us  [per_device(): pl.pallas_call(functools.partial(cost_kernel, dims), out_shape=jax.ShapeD...]
    unnamed x7 -> x6, local copies, waits for them, and re-layouts: 1.61 us -> 0.84 us
where the time goes in v2:
time: 24.1 us; the launch traced here: 23.8 us
  Pallas kernels  23 us (95%)
  local copies, waits for them, and re-layouts  0.84 us (3%)
    pallas_call x1, Pallas kernels, per_device(): pl.pallas_call(functools.partial(cost_kernel, dims), out_shape=jax.ShapeD...  13 us
    pallas_call x1, Pallas kernels, gather_images(): pl.pallas_call(functools.partial(gather_kernel, blocks, cols), out_shape=...  10 us
    unnamed x6, local copies, waits for them, and re-layouts  0.84 us

profile of v2, /device:TPU:0, one launch (start us, length us, event | category | flops | bytes accessed | tf_op | source)
XLA Modules:
  0.0 23.8 jit_solution(4527932199366825938)
XLA Ops:
  0.0 0.0 copy-start.1
  0.0 0.0 copy-start.2
  0.0 10.0 %shard_map.37.gath_ref = bf16[2,4,32,128]{3,2,1,0:T(8,128)(2,1)} custom-call(bf16[32,128]{1,0:T(8,128)(2,1)} %bitcast.3), custom_call_target="tpu_custom_call" | custom-call | tf_op jit(solution)/shard_map/pallas_call | solution.py:55
  10.0 0.0 copy-done.1
  10.0 0.0 copy-done.2
  10.1 0.0 copy-start
  10.1 0.8 %copy-done = bf16[2,4,32,128]{3,2,1,0:T(8,128)(2,1)S(1)} copy-done((bf16[2,4,32,128]{3,2,1,0:T(8,128)(2,1)S(1)}, bf16[2,4,32,128]{3,2,1,0:T(8,128)(2,1)}, u32[]{:S(2)}) %copy-start) | copy-done | bytes 65560
  10.9 13.0 %shard_map.38 = f32[4,32,8,128]{3,2,1,0:T(8,128)} custom-call(bf16[2,4,32,128]{3,2,1,0:T(8,128)(2,1)S(1)} %copy-done, s32[2,64]{1,0:T(2,128)S(1)} %bitcast.2, s32[64]{0:T(128)S(1)} %copy-done.2), custom_call_target="tpu_custom_call" | custom-call | tf_op jit(solution)/shard_map/pallas_call | solution.py:274
Async XLA Ops:
  0.0 10.0 %copy-start.1 = (s32[64,2]{0,1:T(2,128)S(1)}, s32[64,2]{0,1:T(2,128)}, u32[]{:S(2)}) copy-start(s32[64,2]{0,1:T(2,128)} %param.4) | copy-start | bytes 1540
  0.0 10.0 %copy-start.2 = (s32[64]{0:T(128)S(1)}, s32[64]{0:T(128)}, u32[]{:S(2)}) copy-start(s32[64]{0:T(128)} %offs_ref.1) | copy-start | bytes 772
  10.1 0.8 %copy-start = (bf16[2,4,32,128]{3,2,1,0:T(8,128)(2,1)S(1)}, bf16[2,4,32,128]{3,2,1,0:T(8,128)(2,1)}, u32[]{:S(2)}) copy-start(bf16[2,4,32,128]{3,2,1,0:T(8,128)(2,1)} %shard_map.37.gath_ref) | copy-start | bytes 196612

commit v3 on v2

--- a/solution.py
+++ b/solution.py
@@ -54,7 +54,7 @@
     total = blocks * cols
     return pl.pallas_call(
         functools.partial(gather_kernel, blocks, cols),
-        out_shape=jax.ShapeDtypeStruct((cols, blocks, rows, columns), images.dtype),
+        out_shape=pltpu.VMEM((cols, blocks, rows, columns), images.dtype),
         in_specs=[pl.BlockSpec(memory_space=pltpu.VMEM)],
         out_specs=pl.BlockSpec(memory_space=pltpu.VMEM),
         scratch_shapes=[
@@ -75,7 +75,7 @@
 def cost_kernel(
     dims, gath_ref, pairs_ref, offs_ref, out_ref,
     nat, nat_f, nat_m, nat_r, st_g, st_m, st_r, st_f, st_a, st_b,
-    gt, m2t, r2t, ft, m1t, r1t, sel, box, two, four, task_ref,
+    gt, m2t, r2t, ft, m1t, r1t, sel, box, two, task_ref,
 ):
     blocks, cols, views, rows, columns, pair_count, per_sub, batches, folded = dims
     per_batch = LANES // rows
@@ -216,14 +216,12 @@
         costs = {}
         for unit, (batch, part) in enumerate(work):
             disp = step + part * half
-            box_at, two_at, four_at = box.at[buffer, unit], two.at[buffer, unit], four.at[buffer, unit]
+            box_at, two_at = box.at[buffer, unit], two.at[buffer, unit]
             one = sums[unit * span : (unit + 1) * span]
             box_at[0:span, :] = one
-            pair_sum = one + box_at[1 : span + 1, :]
-            two_at[0:span, :] = pair_sum
-            quad = pair_sum + two_at[2 : span + 2, :]
-            four_at[0:span, :] = quad
-            cross = quad[0:columns] + four_at[4 : columns + 4, :] + one[2 * RAD :]
+            triple = one + box_at[1 : span + 1, :] + box_at[2 : span + 2, :]
+            two_at[0:span, :] = triple
+            cross = triple[0:columns] + two_at[3 : columns + 3, :] + two_at[6 : columns + 6, :]
             at = pl.ds(per_sub + RAD - disp, columns)
             gain = r1t[batch] * r2t[batch, at, :]
             cost = 1.0 - (cross - m1t[batch] * m2t[batch, at, :]) * gain
@@ -281,7 +279,7 @@
             stage, stage, stage, stage, narrow, narrow,
             turned, turned, turned, turned, turned_narrow, turned_narrow,
             pltpu.VMEM((2, batches, views * rows, LANES), jnp.bfloat16),
-            work, work, work,
+            work, work,
             pltpu.SMEM((batches * per_batch + 1,), jnp.int32),
         ],
         compiler_params=pltpu.CompilerParams(vmem_limit_bytes=40 * 2**20),

time: 24.1 us -> 22.5 us (0.934)
  local copies, waits for them, and re-layouts: 0.84 us -> 0.01 us
  Pallas kernels: 23 us -> 22.3 us
    unnamed x6 -> x4, local copies, waits for them, and re-layouts: 0.84 us -> 0.01 us
    pallas_call x1, Pallas kernels: 10 us -> 9.41 us  [gather_images(): pl.pallas_call(functools.partial(gather_kernel, blocks, cols), out_shape=...]
where the time goes in v3:
time: 22.5 us; the launch traced here: 22.3 us
  Pallas kernels  22.3 us (99%)
    pallas_call x1, Pallas kernels, per_device(): pl.pallas_call(functools.partial(cost_kernel, dims), out_shape=jax.ShapeD...  12.9 us
    pallas_call x1, Pallas kernels, gather_images(): pl.pallas_call(functools.partial(gather_kernel, blocks, cols), out_shape=...  9.41 us

profile of v3, /device:TPU:0, one launch (start us, length us, event | category | flops | bytes accessed | tf_op | source)
XLA Modules:
  0.0 22.3 jit_solution(17935033152582564237)
XLA Ops:
  0.0 0.0 copy-start
  0.0 0.0 copy-start.1
  0.0 9.4 %shard_map.37.gath_ref = bf16[2,4,32,128]{3,2,1,0:T(8,128)(2,1)S(1)} custom-call(bf16[32,128]{1,0:T(8,128)(2,1)} %bitcast.3), custom_call_target="tpu_custom_call" | custom-call | tf_op jit(solution)/shard_map/pallas_call | solution.py:55
  9.4 0.0 copy-done
  9.4 0.0 copy-done.1
  9.4 12.9 %shard_map.38 = f32[4,32,8,128]{3,2,1,0:T(8,128)} custom-call(bf16[2,4,32,128]{3,2,1,0:T(8,128)(2,1)S(1)} %shard_map.37.gath_ref, s32[2,64]{1,0:T(2,128)S(1)} %bitcast.2, s32[64]{0:T(128)S(1)} %copy-done.1), custom_call_target="tpu_custom_call" | custom-call | tf_op jit(solution)/shard_map/pallas_call | solution.py:272
Async XLA Ops:
  0.0 9.4 %copy-start = (s32[64,2]{0,1:T(2,128)S(1)}, s32[64,2]{0,1:T(2,128)}, u32[]{:S(2)}) copy-start(s32[64,2]{0,1:T(2,128)} %param.4) | copy-start | bytes 1540
  0.0 9.4 %copy-start.1 = (s32[64]{0:T(128)S(1)}, s32[64]{0:T(128)}, u32[]{:S(2)}) copy-start(s32[64]{0:T(128)} %offs_ref.1) | copy-start | bytes 772

commit v4 on v3

--- a/solution.py
+++ b/solution.py
@@ -11,7 +11,7 @@
 RAD = 4
 SMOOTH = 0.01
 LANES = 128
-FOLD = 2
+FOLD = 4
 WIN = 2 * RAD + 1
 MESH = pl.DeviceIdType.MESH
 
@@ -83,6 +83,7 @@
     slots = batches * per_batch
     all_rows = blocks * views * rows
     wide = 4 * columns
+    three = 3 * columns
     my_view = lax.axis_index("views")
     my_col = lax.axis_index("cols")
     sub_start = lax.axis_index("sub") * per_sub
@@ -127,12 +128,12 @@
         pair_sum = sums + pltpu.roll(sums, 1, 1)
         quad = pair_sum + pltpu.roll(pair_sum, 2, 1)
         octo = quad + pltpu.roll(quad, 4, 1)
-        return pltpu.roll(octo + pltpu.roll(sums, 8, 1), wide - RAD, 1)
+        return octo + pltpu.roll(sums, 8, 1)
 
     for chunk in range(all_rows // LANES):
         span = slice(chunk * LANES, (chunk + 1) * LANES)
-        tile = nat[span, :]
-        nat_f[span, :] = pltpu.roll(tile, 2 * columns + RAD, 1)[:, : 2 * columns]
+        tile = pltpu.roll(nat[span, :], wide - RAD, 1)[:, :three]
+        nat_f[span, :] = tile[:, columns:]
         mean = across(
             jnp.dot(band, tile.astype(jnp.bfloat16), preferred_element_type=jnp.float32)
         ) * scale
@@ -149,7 +150,6 @@
     view_row = lax.broadcasted_iota(jnp.int32, (views * rows, LANES), 0)
 
     half = per_sub // 2
-    three = 3 * columns
     target = view_row // rows
     same_row = lax.rem(slot_lane, rows) == lax.rem(view_row, rows)
 
@@ -209,7 +209,7 @@
         for batch, part in work:
             disp = step + part * half
             parts.append(
-                split_exact(ft[batch, 0:span, :] * gt[batch, pl.ds(per_sub - disp, span), :])
+                split_exact(ft[batch, 2 * columns - span :, :] * gt[batch, pl.ds(per_sub - disp, span), :])
             )
         stacked = jnp.concatenate([jnp.concatenate(pair, axis=1) for pair in parts], axis=0)
         sums = jnp.dot(stacked, band_tall, preferred_element_type=jnp.float32)
@@ -267,6 +267,7 @@
     turned_narrow = pltpu.VMEM((batches, columns, LANES), f32)
     work = pltpu.VMEM((FOLD, units, span + 8, LANES), f32)
     whole = pltpu.VMEM((all_rows, 4 * columns), f32)
+    trio = pltpu.VMEM((all_rows, 3 * columns), f32)
     smem = pl.BlockSpec(memory_space=pltpu.SMEM)
     vmem = pl.BlockSpec(memory_space=pltpu.VMEM)
     return pl.pallas_call(
@@ -275,7 +276,7 @@
         in_specs=[vmem, smem, smem],
         out_specs=vmem,
         scratch_shapes=[
-            whole, pltpu.VMEM((all_rows, 2 * columns), f32), whole, whole,
+            whole, pltpu.VMEM((all_rows, 2 * columns), f32), trio, trio,
             stage, stage, stage, stage, narrow, narrow,
             turned, turned, turned, turned, turned_narrow, turned_narrow,
             pltpu.VMEM((2, batches, views * rows, LANES), jnp.bfloat16),

time: 22.5 us -> 21.5 us (0.956)
  Pallas kernels: 22.3 us -> 21.3 us
    pallas_call x1, Pallas kernels: 12.9 us -> 11.9 us  [per_device(): pl.pallas_call(functools.partial(cost_kernel, dims), out_shape=jax.ShapeD...]
where the time goes in v4:
time: 21.5 us; the launch traced here: 21.3 us
  Pallas kernels  21.3 us (99%)
    pallas_call x1, Pallas kernels, per_device(): pl.pallas_call(functools.partial(cost_kernel, dims), out_shape=jax.ShapeD...  11.9 us
    pallas_call x1, Pallas kernels, gather_images(): pl.pallas_call(functools.partial(gather_kernel, blocks, cols), out_shape=...  9.41 us

profile of v4, /device:TPU:0, one launch (start us, length us, event | category | flops | bytes accessed | tf_op | source)
XLA Modules:
  0.0 21.3 jit_solution(18189063880689593566)
XLA Ops:
  0.0 0.0 copy-start
  0.0 0.0 copy-start.1
  0.0 9.4 %shard_map.37.gath_ref = bf16[2,4,32,128]{3,2,1,0:T(8,128)(2,1)S(1)} custom-call(bf16[32,128]{1,0:T(8,128)(2,1)} %bitcast.3), custom_call_target="tpu_custom_call" | custom-call | tf_op jit(solution)/shard_map/pallas_call | solution.py:55
  9.4 0.0 copy-done
  9.4 0.0 copy-done.1
  9.4 11.9 %shard_map.38 = f32[4,32,8,128]{3,2,1,0:T(8,128)} custom-call(bf16[2,4,32,128]{3,2,1,0:T(8,128)(2,1)S(1)} %shard_map.37.gath_ref, s32[2,64]{1,0:T(2,128)S(1)} %bitcast.2, s32[64]{0:T(128)S(1)} %copy-done.1), custom_call_target="tpu_custom_call" | custom-call | tf_op jit(solution)/shard_map/pallas_call | solution.py:273
Async XLA Ops:
  0.0 9.4 %copy-start = (s32[64,2]{0,1:T(2,128)S(1)}, s32[64,2]{0,1:T(2,128)}, u32[]{:S(2)}) copy-start(s32[64,2]{0,1:T(2,128)} %param.4) | copy-start | bytes 1540
  0.0 9.4 %copy-start.1 = (s32[64]{0:T(128)S(1)}, s32[64]{0:T(128)}, u32[]{:S(2)}) copy-start(s32[64]{0:T(128)} %offs_ref.1) | copy-start | bytes 772

commit v5 on v4

--- a/solution.py
+++ b/solution.py
@@ -170,12 +170,12 @@
             if late:
                 start = start - half
             turn = three - start
-            st_g[here, :] = pltpu.roll(nat[second_at, :three], turn, 1)[:, : 2 * columns]
-            st_m[here, :] = pltpu.roll(nat_m[second_at, :three], turn, 1)[:, : 2 * columns]
-            st_r[here, :] = pltpu.roll(nat_r[second_at, :three], turn, 1)[:, : 2 * columns]
-            st_f[here, :] = nat_f[first_at, :]
-            st_a[here, :] = nat_m[first_at, 2 * columns : three]
-            st_b[here, :] = nat_r[first_at, 2 * columns : three]
+            st_g[batch, here, :] = pltpu.roll(nat[second_at, :three], turn, 1)[:, : 2 * columns]
+            st_m[batch, here, :] = pltpu.roll(nat_m[second_at, :three], turn, 1)[:, : 2 * columns]
+            st_r[batch, here, :] = pltpu.roll(nat_r[second_at, :three], turn, 1)[:, : 2 * columns]
+            st_f[batch, here, :] = nat_f[first_at, :]
+            st_a[batch, here, :] = nat_m[first_at, 2 * columns : three]
+            st_b[batch, here, :] = nat_r[first_at, 2 * columns : three]
             mine = (slot_lane // rows) == slot
             first_of = jnp.where(mine, jnp.where(live, first - base, -1), first_of)
             second_of = jnp.where(mine, jnp.where(live, second - base, -1), second_of)
@@ -184,20 +184,15 @@
         for part in range(2):
             chosen = hit & (early if part == 0 else jnp.logical_not(early)) if fold else hit
             sel[part, batch] = chosen.astype(jnp.float32).astype(jnp.bfloat16)
-        gt[batch] = st_g[...].T
-        m2t[batch] = st_m[...].T
-        r2t[batch] = st_r[...].T
-        ft[batch] = st_f[...].T
-        m1t[batch] = st_a[...].T * float(WIN * WIN)
-        r1t[batch] = st_b[...].T * scale
-
-    def prepare_full(batch, carry):
-        prepare(batch, False)
-        return carry
-
-    lax.fori_loop(0, batches - int(folded), prepare_full, 0)
-    if folded:
-        prepare(batches - 1, True)
+        gt[batch] = st_g[batch].T
+        m2t[batch] = st_m[batch].T
+        r2t[batch] = st_r[batch].T
+        ft[batch] = st_f[batch].T
+        m1t[batch] = st_a[batch].T * float(WIN * WIN)
+        r1t[batch] = st_b[batch].T * scale
+
+    for batch in range(batches):
+        prepare(batch, folded and batch == batches - 1)
 
     span = columns + 2 * RAD
     work = [(batch, part) for part in range(2) for batch in range(batches)]
@@ -211,13 +206,13 @@
             parts.append(
                 split_exact(ft[batch, 2 * columns - span :, :] * gt[batch, pl.ds(per_sub - disp, span), :])
             )
-        stacked = jnp.concatenate([jnp.concatenate(pair, axis=1) for pair in parts], axis=0)
-        sums = jnp.dot(stacked, band_tall, preferred_element_type=jnp.float32)
         costs = {}
         for unit, (batch, part) in enumerate(work):
             disp = step + part * half
             box_at, two_at = box.at[buffer, unit], two.at[buffer, unit]
-            one = sums[unit * span : (unit + 1) * span]
+            one = jnp.dot(
+                jnp.concatenate(parts[unit], axis=1), band_tall, preferred_element_type=jnp.float32
+            )
             box_at[0:span, :] = one
             triple = one + box_at[1 : span + 1, :] + box_at[2 : span + 2, :]
             two_at[0:span, :] = triple
@@ -261,8 +256,8 @@
     all_rows = blocks * views * rows
     span = columns + 2 * RAD
     f32 = jnp.float32
-    stage = pltpu.VMEM((LANES, 2 * columns), f32)
-    narrow = pltpu.VMEM((LANES, columns), f32)
+    stage = pltpu.VMEM((batches, LANES, 2 * columns), f32)
+    narrow = pltpu.VMEM((batches, LANES, columns), f32)
     turned = pltpu.VMEM((batches, 2 * columns, LANES), f32)
     turned_narrow = pltpu.VMEM((batches, columns, LANES), f32)
     work = pltpu.VMEM((FOLD, units, span + 8, LANES), f32)

time: 21.5 us -> 19.8 us (0.921)
  Pallas kernels: 21.3 us -> 19.6 us
    pallas_call x1, Pallas kernels: 11.9 us -> 10.2 us  [per_device(): pl.pallas_call(functools.partial(cost_kernel, dims), out_shape=jax.ShapeD...]
where the time goes in v5:
time: 19.8 us; the launch traced here: 19.7 us
  Pallas kernels  19.6 us (99%)
    pallas_call x1, Pallas kernels, per_device(): pl.pallas_call(functools.partial(cost_kernel, dims), out_shape=jax.ShapeD...  10.2 us
    pallas_call x1, Pallas kernels, gather_images(): pl.pallas_call(functools.partial(gather_kernel, blocks, cols), out_shape=...  9.41 us

profile of v5, /device:TPU:0, one launch (start us, length us, event | category | flops | bytes accessed | tf_op | source)
XLA Modules:
  0.0 19.7 jit_solution(11292634448639527707)
XLA Ops:
  0.0 0.0 copy-start
  0.0 0.0 copy-start.1
  0.0 9.4 %shard_map.37.gath_ref = bf16[2,4,32,128]{3,2,1,0:T(8,128)(2,1)S(1)} custom-call(bf16[32,128]{1,0:T(8,128)(2,1)} %bitcast.3), custom_call_target="tpu_custom_call" | custom-call | tf_op jit(solution)/shard_map/pallas_call | solution.py:55
  9.4 0.0 copy-done
  9.4 0.0 copy-done.1
  9.4 10.2 %shard_map.38 = f32[4,32,8,128]{3,2,1,0:T(8,128)} custom-call(bf16[2,4,32,128]{3,2,1,0:T(8,128)(2,1)S(1)} %shard_map.37.gath_ref, s32[2,64]{1,0:T(2,128)S(1)} %bitcast.2, s32[64]{0:T(128)S(1)} %copy-done.1), custom_call_target="tpu_custom_call" | custom-call | tf_op jit(solution)/shard_map/pallas_call | solution.py:268
Async XLA Ops:
  0.0 9.4 %copy-start = (s32[64,2]{0,1:T(2,128)S(1)}, s32[64,2]{0,1:T(2,128)}, u32[]{:S(2)}) copy-start(s32[64,2]{0,1:T(2,128)} %param.4) | copy-start | bytes 1540
  0.0 9.4 %copy-start.1 = (s32[64]{0:T(128)S(1)}, s32[64]{0:T(128)}, u32[]{:S(2)}) copy-start(s32[64]{0:T(128)} %offs_ref.1) | copy-start | bytes 772

commit v6 on v5

--- a/solution.py
+++ b/solution.py
@@ -11,7 +11,7 @@
 RAD = 4
 SMOOTH = 0.01
 LANES = 128
-FOLD = 4
+FOLD = 8
 WIN = 2 * RAD + 1
 MESH = pl.DeviceIdType.MESH
 
@@ -200,18 +200,13 @@
         work.remove((batches - 1, 1))
 
     def score(step, buffer):
-        parts = []
-        for batch, part in work:
-            disp = step + part * half
-            parts.append(
-                split_exact(ft[batch, 2 * columns - span :, :] * gt[batch, pl.ds(per_sub - disp, span), :])
-            )
         costs = {}
         for unit, (batch, part) in enumerate(work):
             disp = step + part * half
             box_at, two_at = box.at[buffer, unit], two.at[buffer, unit]
+            product = ft[batch, 2 * columns - span :, :] * gt[batch, pl.ds(per_sub - disp, span), :]
             one = jnp.dot(
-                jnp.concatenate(parts[unit], axis=1), band_tall, preferred_element_type=jnp.float32
+                jnp.concatenate(split_exact(product), axis=1), band_tall, preferred_element_type=jnp.float32
             )
             box_at[0:span, :] = one
             triple = one + box_at[1 : span + 1, :] + box_at[2 : span + 2, :]

time: 19.8 us -> 19.5 us (0.985)
  Pallas kernels: 19.6 us -> 19.4 us
    pallas_call x1, Pallas kernels: 10.2 us -> 9.95 us  [per_device(): pl.pallas_call(functools.partial(cost_kernel, dims), out_shape=jax.ShapeD...]
where the time goes in v6:
time: 19.5 us; the launch traced here: 19.4 us
  Pallas kernels  19.4 us (99%)
    pallas_call x1, Pallas kernels, per_device(): pl.pallas_call(functools.partial(cost_kernel, dims), out_shape=jax.ShapeD...  9.95 us
    pallas_call x1, Pallas kernels, gather_images(): pl.pallas_call(functools.partial(gather_kernel, blocks, cols), out_shape=...  9.41 us

profile of v6, /device:TPU:0, one launch (start us, length us, event | category | flops | bytes accessed | tf_op | source)
XLA Modules:
  0.0 19.4 jit_solution(15951059533071623241)
XLA Ops:
  0.0 0.0 copy-start
  0.0 0.0 copy-start.1
  0.0 9.4 %shard_map.37.gath_ref = bf16[2,4,32,128]{3,2,1,0:T(8,128)(2,1)S(1)} custom-call(bf16[32,128]{1,0:T(8,128)(2,1)} %bitcast.3), custom_call_target="tpu_custom_call" | custom-call | tf_op jit(solution)/shard_map/pallas_call | solution.py:55
  9.4 0.0 copy-done
  9.4 0.0 copy-done.1
  9.4 9.9 %shard_map.38 = f32[4,32,8,128]{3,2,1,0:T(8,128)} custom-call(bf16[2,4,32,128]{3,2,1,0:T(8,128)(2,1)S(1)} %shard_map.37.gath_ref, s32[2,64]{1,0:T(2,128)S(1)} %bitcast.2, s32[64]{0:T(128)S(1)} %copy-done.1), custom_call_target="tpu_custom_call" | custom-call | tf_op jit(solution)/shard_map/pallas_call | solution.py:263
Async XLA Ops:
  0.0 9.4 %copy-start = (s32[64,2]{0,1:T(2,128)S(1)}, s32[64,2]{0,1:T(2,128)}, u32[]{:S(2)}) copy-start(s32[64,2]{0,1:T(2,128)} %param.4) | copy-start | bytes 1540
  0.0 9.4 %copy-start.1 = (s32[64]{0:T(128)S(1)}, s32[64]{0:T(128)}, u32[]{:S(2)}) copy-start(s32[64]{0:T(128)} %offs_ref.1) | copy-start | bytes 772
